TPU v7x, 32 devices: a whole 2x2x4 slice. The times are simulated.
32 devices in a mesh: dp: 8 (over z, core), tensor: 4 (over y, x).
Axes of the slice: x: 2, y: 2, z: 4, core: 2. Of those that a mesh axis runs over, the one named last changes fastest.
Arguments:
- teacher_queries: bfloat16 [8, 512, 8192], P('dp', None, 'tensor'), may hold values from -100 to 100
- teacher_keys: bfloat16 [8, 512, 1024], P('dp', None, 'tensor'), may hold values from -5 to 5
- teacher_values: bfloat16 [8, 512, 1024], P('dp', None, 'tensor'), may hold values from -6 to 6
- projector: bfloat16 [8192, 4096], P('tensor'), may hold values from -0.25 to 0.25
- student_inputs: bfloat16 [8, 512, 4096], P('dp', 'tensor'), may hold values from -30 to 30
- query_weight: bfloat16 [4096, 4096], P('dp', 'tensor'), may hold values from -1 to 1
- key_weight: bfloat16 [4096, 1024], P('dp', 'tensor'), may hold values from -1 to 1
- value_weight: bfloat16 [4096, 1024], P('dp', 'tensor'), may hold values from -0.09375 to 0.09375
Outputs:
- query_grad: float32 [4096, 4096], P('dp', 'tensor')
- key_grad: float32 [4096, 1024], P('dp', 'tensor')
- value_grad: float32 [4096, 1024], P('dp', 'tensor')
All inputs are finite; a program needn't handle non-finite values.
Results may differ from a plain program's by a relative error of at most 0.029.
Values may be sent and summed in bfloat16 or wider, within the bound.
A program may use at most 128 MiB of HBM per device.

v0:
```python
import jax
import jax.numpy as jnp
from jax import lax
from jax.sharding import PartitionSpec as P

HEAD = 128
TQH = 64
TKVH = 8
SQH = 32
SKVH = 8


def attend(queries, keys, values, groups, factor):
    length = queries.shape[0]
    heads_kv = keys.shape[1] // HEAD
    query_heads = queries.reshape(length, heads_kv, groups, HEAD)
    key_heads = keys.reshape(length, heads_kv, HEAD)
    value_heads = values.reshape(length, heads_kv, HEAD)
    block_rows = min(512, length)
    pieces = []
    kept = []
    for number in range(length // block_rows):
        first = number * block_rows
        limit = first + block_rows
        scores = (
            jnp.einsum(
                "qhgd,khd->hgqk",
                query_heads[first:limit],
                key_heads[:limit],
                preferred_element_type=jnp.float32,
            )
            * factor
        )
        visible = jnp.arange(limit)[None, :] <= (first + jnp.arange(block_rows))[:, None]
        scores = jnp.where(visible, scores, -1e30)
        shifted = jnp.exp(scores - jnp.max(scores, axis=-1, keepdims=True))
        probs = shifted / jnp.sum(shifted, axis=-1, keepdims=True)
        rounded = probs.astype(jnp.bfloat16)
        context = jnp.einsum(
            "hgqk,khd->qhgd", rounded, value_heads[:limit], preferred_element_type=jnp.float32
        )
        pieces.append(context.reshape(block_rows, -1))
        kept.append(probs)
    return (jnp.concatenate(pieces, axis=0), kept)


def attend_back(incoming_all, queries, keys, values, kept, groups, factor):
    length = queries.shape[0]
    heads_kv = keys.shape[1] // HEAD
    query_heads = queries.reshape(length, heads_kv, groups, HEAD)
    key_heads = keys.reshape(length, heads_kv, HEAD)
    value_heads = values.reshape(length, heads_kv, HEAD)
    block_rows = min(512, length)
    grad_keys = jnp.zeros((length, heads_kv, HEAD), jnp.float32)
    grad_values = jnp.zeros((length, heads_kv, HEAD), jnp.float32)
    query_parts = []
    for number in range(length // block_rows):
        first = number * block_rows
        limit = first + block_rows
        probs = kept[number]
        rounded = probs.astype(jnp.bfloat16)
        incoming = incoming_all[first:limit].reshape(block_rows, heads_kv, groups, HEAD)
        grad_values = grad_values.at[:limit].add(
            jnp.einsum("hgqk,qhgd->khd", rounded, incoming, preferred_element_type=jnp.float32)
        )
        grad_probs = jnp.einsum(
            "qhgd,khd->hgqk", incoming, value_heads[:limit], preferred_element_type=jnp.float32
        )
        grad_scores = probs * (grad_probs - jnp.sum(grad_probs * probs, axis=-1, keepdims=True))
        scaled = (grad_scores * factor).astype(jnp.bfloat16)
        query_parts.append(
            jnp.einsum(
                "hgqk,khd->qhgd", scaled, key_heads[:limit], preferred_element_type=jnp.float32
            ).reshape(block_rows, -1)
        )
        grad_keys = grad_keys.at[:limit].add(
            jnp.einsum(
                "hgqk,qhgd->khd",
                scaled,
                query_heads[first:limit],
                preferred_element_type=jnp.float32,
            )
        )
    grad_queries = jnp.concatenate(query_parts, axis=0).astype(jnp.bfloat16)
    return (
        grad_queries,
        grad_keys.reshape(length, -1).astype(jnp.bfloat16),
        grad_values.reshape(length, -1).astype(jnp.bfloat16),
    )


def per_device(
    teacher_queries,
    teacher_keys,
    teacher_values,
    projector,
    student_inputs,
    query_weight,
    key_weight,
    value_weight,
):
    factor = HEAD ** (-0.5)
    dp_count = lax.axis_size("dp")
    context_t, unused = attend(
        teacher_queries[0], teacher_keys[0], teacher_values[0], TQH // TKVH, factor
    )
    context_t = context_t.astype(jnp.bfloat16)
    summed = lax.psum_scatter(
        lax.dot_general(
            projector, context_t, (((0,), (1,)), ((), ())), preferred_element_type=jnp.float32
        ).astype(jnp.bfloat16),
        "tensor",
        scatter_dimension=0,
        tiled=True,
    ).astype(jnp.float32)
    target = summed.T
    rows_all = lax.all_gather(student_inputs[0], "tensor", axis=0, tiled=True)
    full_weights = (
        lax.all_gather(query_weight, "dp", axis=0, tiled=True),
        lax.all_gather(key_weight, "dp", axis=0, tiled=True),
        lax.all_gather(value_weight, "dp", axis=0, tiled=True),
    )
    rows_all, full_weights = (rows_all, full_weights)
    queries = jnp.dot(rows_all, full_weights[0], preferred_element_type=jnp.float32).astype(
        jnp.bfloat16
    )
    keys = jnp.dot(rows_all, full_weights[1], preferred_element_type=jnp.float32).astype(
        jnp.bfloat16
    )
    values = jnp.dot(rows_all, full_weights[2], preferred_element_type=jnp.float32).astype(
        jnp.bfloat16
    )
    context_s, kept = attend(queries, keys, values, SQH // SKVH, factor)
    grad_context = ((context_s - target) / dp_count).astype(jnp.bfloat16)
    grad_q, grad_k, grad_v = attend_back(
        grad_context, queries, keys, values, kept, SQH // SKVH, factor
    )
    grad_all = jnp.concatenate([grad_q, grad_k, grad_v], axis=1)
    whole = lax.dot_general(
        rows_all, grad_all, (((0,), (0,)), ((), ())), preferred_element_type=jnp.float32
    )
    reduced = lax.psum_scatter(
        whole.astype(jnp.bfloat16), "dp", scatter_dimension=0, tiled=True
    ).astype(jnp.float32)
    query_cols = query_weight.shape[1]
    key_cols = key_weight.shape[1]
    return (
        reduced[:, :query_cols],
        reduced[:, query_cols : query_cols + key_cols],
        reduced[:, query_cols + key_cols :],
    )


def solution(mesh):
    placed = (
        P("dp", None, "tensor"),
        P("dp", None, "tensor"),
        P("dp", None, "tensor"),
        P("tensor", None),
        P("dp", "tensor", None),
        P("dp", "tensor"),
        P("dp", "tensor"),
        P("dp", "tensor"),
    )
    return jax.shard_map(
        per_device,
        mesh=mesh,
        in_specs=placed,
        out_specs=(P("dp", "tensor"), P("dp", "tensor"), P("dp", "tensor")),
        check_vma=False,
    )
```

profile of v0, /device:TPU:0, one launch (start us, length us, event | category | flops | bytes accessed | tf_op | source)
XLA Modules:
  0.0 455.6 jit_solution(9326126580650601653)
XLA Ops:
  10.0 2.2 copy.51
  14.4 8.3 %fusion.29 = f32[2,512,512,8]{2,1,3,0:T(8,128)} fusion(bf16[512,2,8,128]{3,2,1,0:T(8,128)(2,1)S(1)} %bitcast.150, bf16[512,2,128,1]{2,1,0,3:T(2,128)(2,1)S(1)} %bitcast.155), kind=kOutput, calls=%fused_computation.40 | convolution fusion | flops 1073741824 | bytes 19136512 | tf_op jit(solution)/shard_map/qhgd,khd->hgqk/dot_general | solution.py:26
  22.7 18.1 %fusion.73 = (f32[2,8,512]{2,1,0:T(8,128)S(1)}, f32[2,8,512,512]{2,3,1,0:T(8,128)}) fusion(f32[2,512,512,8]{2,1,3,0:T(8,128)} %fusion.29, pred[512,512]{0,1:T(8,128)(4,1)S(1)} %iota_compare_fusion), kind=kOutput, calls=%fused_computation.74 | output fusion | flops 25166336 | bytes 33849344 | tf_op jit(solution)/shard_map/sub | solution.py:36
  40.8 7.1 %fusion.35 = bf16[2,8,512,128]{2,3,1,0:T(8,128)(2,1)S(1)} fusion(bf16[512,2,128,1]{0,2,3,1:T(8,128)(2,1)S(1)} %bitcast.160, f32[2,8,512,512]{2,3,1,0:T(8,128)} %get-tuple-element.51, f32[2,8,512]{2,1,0:T(8,128)S(1)} %get-tuple-element.50), kind=kOutput, calls=%fused_computation.46 | convolution fusion | flops 1083179008 | bytes 19169280 | tf_op jit(solution)/shard_map/hgqk,khd->qhgd/dot_general | solution.py:39
  47.9 14.8 %fusion.13 = bf16[4096,512]{0,1:T(8,128)(2,1)} fusion(bf16[512,2048]{0,1:T(8,128)(2,1)S(1)} %bitcast.161, bf16[2048,4096]{1,0:T(8,128)(2,1)} %param.19), kind=kOutput, calls=%fused_computation.22 | convolution fusion | flops 8592031744 | bytes 23068672 | tf_op jit(solution)/shard_map/dot_general | solution.py:109
  63.0 32.5 %all-gather.12.cloned.1.call-done = bf16[1,512,4096]{2,1,0:T(8,128)(2,1)} async-done(((bf16[1,128,4096]{2,1,0:T(8,128)(2,1)}), bf16[1,512,4096]{2,1,0:T(8,128)(2,1)}) %all-gather.12.cloned.1.call-update) | async-done | bytes 4194320 | tf_op jit(solution)/shard_map/all_gather | solution.py:117
  95.5 4.2 fusion.53
  99.7 26.6 %all-gather.10.cloned.1.call-done = bf16[4096,256]{1,0:T(8,128)(2,1)} async-done(((bf16[512,256]{1,0:T(8,128)(2,1)}), bf16[4096,256]{1,0:T(8,128)(2,1)}) %all-gather.10.cloned.1.call-update) | async-done | bytes 2097168 | tf_op jit(solution)/shard_map/all_gather | solution.py:121
  126.2 4.2 fusion.56
  130.4 78.9 %all-gather.8.cloned.1.call-done = bf16[4096,1024]{1,0:T(8,128)(2,1)} async-done(((bf16[512,1024]{1,0:T(8,128)(2,1)}), bf16[4096,1024]{1,0:T(8,128)(2,1)}) %all-gather.8.cloned.1.call-update) | async-done | bytes 8388624 | tf_op jit(solution)/shard_map/all_gather | solution.py:119
  209.3 9.1 %fusion.41 = bf16[512,1024]{1,0:T(8,128)(2,1)S(1)} fusion(bf16[4096,1024]{1,0:T(8,128)(2,1)} %all-gather.8.cloned.1.call-done, bf16[1,512,4096]{2,1,0:T(8,128)(2,1)} %all-gather.12.cloned.1.call-done), kind=kOutput, calls=%fused_computation.52 | convolution fusion | flops 4295491584 | bytes 13631488 | tf_op jit(solution)/shard_map/dot_general | solution.py:124
  219.0 5.4 %fusion.72 = (f32[2,4,512]{2,1,0:T(4,128)S(1)}, f32[2,4,512,512]{2,3,1,0:T(8,128)}) fusion(pred[512,512]{0,1:T(8,128)(4,1)S(1)} %iota_compare_fusion, bf16[512,2,128,1]{0,2,3,1:T(8,128)(2,1)S(1)} %bitcast.163, bf16[512,2,4,128]{0,3,2,1:T(8,128)(2,1)S(1)} %bitcast.156), kind=kOutput, calls=%fused_computation.73 | convolution fusion | flops 545260032 | bytes 9977856 | tf_op jit(solution)/shard_map/sub | solution.py:36
  224.4 5.7 %fusion.33 = f32[2,128,4,512]{3,1,2,0:T(8,128)} fusion(bf16[512,2,128,1]{0,2,3,1:T(8,128)(2,1)S(1)} %bitcast.158, f32[2,4,512,512]{2,3,1,0:T(8,128)} %get-tuple-element.49, f32[2,4,512]{2,1,0:T(4,128)S(1)} %get-tuple-element.48), kind=kOutput, calls=%fused_computation.44 | convolution fusion | flops 541065216 | bytes 10764288 | tf_op jit(solution)/shard_map/hgqk,khd->qhgd/dot_general | solution.py:39
  230.1 1.9 copy.18
  232.0 31.3 %reduce-scatter.3.cloned.1.call-done = bf16[1024,512]{0,1:T(8,128)(2,1)} async-done(((bf16[4096,512]{0,1:T(8,128)(2,1)}), bf16[1024,512]{0,1:T(8,128)(2,1)}) %reduce-scatter.3.cloned.1.call-update) | async-done | bytes 1048592 | tf_op jit(solution)/shard_map/reduce_scatter | solution.py:108
  263.3 1.6 fusion.28
  265.5 4.5 fusion.74
  270.0 14.4 %fusion.44 = bf16[2,128,4,512]{3,1,2,0:T(8,128)(2,1)S(1)} fusion(bf16[512,2,128,1]{0,2,3,1:T(8,128)(2,1)} %bitcast.164, f32[2,512,512,4]{2,1,3,0:T(8,128)} %fusion.74, f32[2,4,512,512]{2,3,1,0:T(8,128)} %get-tuple-element.49, f32[2,4,512]{2,1,0:T(4,128)S(1)} %get-tuple-element.48), kind=kOutput, calls=%fused_computation.53 | convolution fusion | flops 552079872 | bytes 18104320 | tf_op jit(solution)/shard_map/hgqk,khd->qhgd/dot_general | solution.py:72
  284.4 12.1 %fusion.49 = bf16[2,128,512]{2,1,0:T(8,128)(2,1)S(1)} fusion(bf16[512,2,4,128]{0,3,2,1:T(8,128)(2,1)S(1)} %bitcast.157, f32[2,512,512,4]{2,1,3,0:T(8,128)} %fusion.74, f32[2,4,512,512]{2,3,1,0:T(8,128)} %get-tuple-element.49, f32[2,4,512]{2,1,0:T(4,128)S(1)} %get-tuple-element.48), kind=kOutput, calls=%fused_computation.56 | convolution fusion | flops 551686656 | bytes 18104320 | tf_op jit(solution)/shard_map/hgqk,qhgd->khd/dot_general | solution.py:77
  296.5 5.0 %fusion.50 = bf16[2,128,512]{2,1,0:T(8,128)(2,1)S(1)} fusion(bf16[512,2,4,128]{0,3,2,1:T(8,128)(2,1)S(1)} %bitcast.152, f32[2,4,512,512]{2,3,1,0:T(8,128)} %get-tuple-element.49, f32[2,4,512]{2,1,0:T(4,128)S(1)} %get-tuple-element.48), kind=kOutput, calls=%fused_computation.57 | convolution fusion | flops 541196288 | bytes 9715712 | tf_op jit(solution)/shard_map/hgqk,qhgd->khd/dot_general | solution.py:64
  301.5 11.3 %fusion.3 = bf16[4096,1536]{0,1:T(8,128)(2,1)} fusion(bf16[1,512,4096]{2,1,0:T(8,128)(2,1)S(1)} %copy-done.2, bf16[512,256]{0,1:T(8,128)(2,1)S(1)} %bitcast.166, bf16[512,256]{0,1:T(8,128)(2,1)S(1)} %bitcast.165, bf16[512,1024]{0,1:T(8,128)(2,1)S(1)} %bitcast.162), kind=kOutput, calls=%fused_computation.7 | convolution fusion | flops 6453460992 | bytes 18350080 | tf_op jit(solution)/shard_map/dot_general | solution.py:139
  312.9 129.4 %reduce-scatter.5.cloned.1.call-done = bf16[512,1536]{0,1:T(8,128)(2,1)} async-done(((bf16[4096,1536]{0,1:T(8,128)(2,1)}), bf16[512,1536]{0,1:T(8,128)(2,1)}) %reduce-scatter.5.cloned.1.call-update) | async-done | bytes 1572880 | tf_op jit(solution)/shard_map/reduce_scatter | solution.py:142
  442.3 1.5 slice.50
  443.8 1.8 copy.26
  (29 shorter events, 9.5 us)
Async XLA Ops:
  7.2 55.8 %all-gather.6.cloned.1.call-start = ((), (), s32[]{:S(2)}) async-start(), calls=%async_computation.2 | async-start | bytes 2359296 | tf_op jit(solution)/shard_map/all_gather | solution.py:120
  7.9 87.6 %all-gather.12.cloned.1.call-start = ((), (), s32[]{:S(2)}) async-start(), calls=%async_computation.7 | async-start | bytes 5242880 | tf_op jit(solution)/shard_map/all_gather | solution.py:117
  8.6 117.6 %all-gather.10.cloned.1.call-start = ((), (), s32[]{:S(2)}) async-start(), calls=%async_computation.4 | async-start | bytes 2359296 | tf_op jit(solution)/shard_map/all_gather | solution.py:121
  9.4 199.9 %all-gather.8.cloned.1.call-start = ((), (), s32[]{:S(2)}) async-start(), calls=%async_computation.3 | async-start | bytes 9437184 | tf_op jit(solution)/shard_map/all_gather | solution.py:119
  10.0 253.4 %reduce-scatter.3.cloned.1.call-start = ((), (), s32[]{:S(2)}) async-start(), calls=%async_computation.5 | async-start | bytes 5242880 | tf_op jit(solution)/shard_map/reduce_scatter | solution.py:108
  62.7 379.5 %reduce-scatter.5.cloned.1.call-start = ((), (), s32[]{:S(2)}) async-start(), calls=%async_computation.6 | async-start | bytes 14155776 | tf_op jit(solution)/shard_map/reduce_scatter | solution.py:142
  99.7 119.3 %copy-start.3 = (bf16[512,256]{0,1:T(8,128)(2,1)}, bf16[512,256]{0,1:T(8,128)(2,1)S(1)}, u32[]{:S(2)}) copy-start(bf16[512,256]{0,1:T(8,128)(2,1)S(1)} %fusion.53) | copy-start | bytes 786436
  219.0 11.1 %copy-start = (bf16[512,1024]{0,1:T(8,128)(2,1)}, bf16[512,1024]{0,1:T(8,128)(2,1)S(1)}, u32[]{:S(2)}) copy-start(bf16[512,1024]{0,1:T(8,128)(2,1)S(1)} %copy.49) | copy-start | bytes 3145732
  270.0 14.4 %copy-start.1 = (bf16[512,1024]{0,1:T(8,128)(2,1)S(1)}, bf16[512,1024]{0,1:T(8,128)(2,1)}, u32[]{:S(2)}) copy-start(bf16[512,1024]{0,1:T(8,128)(2,1)} %copy-done) | copy-start | bytes 3145732
  296.5 5.0 %copy-start.2 = (bf16[1,512,4096]{2,1,0:T(8,128)(2,1)S(1)}, bf16[1,512,4096]{2,1,0:T(8,128)(2,1)}, u32[]{:S(2)}) copy-start(bf16[1,512,4096]{2,1,0:T(8,128)(2,1)} %all-gather.12.cloned.1.call-done) | copy-start | bytes 12582916
Sparse Core Ops, SparseCore 0:
  9.6 31.7 all-gather.5
  43.3 52.1 all-gather.11
  97.1 29.0 all-gather.9
  127.7 81.5 all-gather.7
  212.1 51.1 reduce-scatter.2
  313.0 129.1 reduce-scatter.4
where the time goes:
time: 456 us
  waiting for transfers between devices  301 us (66%)
  matrix products  106 us (23%)
  other arithmetic  19.8 us (4%)
  between operations  14.3 us (3%)
  local copies, waits for them, and re-layouts  13.8 us (3%)
    reduce_scatter x1, waiting for transfers between devices, per_device(): lax.psum_scatter(whole.astype(jnp.bfloat16), 'dp', scatter_dimension=0, t...  129 us
    all_gather x1, waiting for transfers between devices, per_device(): lax.all_gather(query_weight, 'dp', axis=0, tiled=True)  78.9 us
    all_gather x1, waiting for transfers between devices, per_device(): rows_all = lax.all_gather(student_inputs[0], 'tensor', axis=0, tiled=True)  32.5 us
    reduce_scatter x1, waiting for transfers between devices, per_device(): lax.psum_scatter(lax.dot_general(projector, context_t, (((0,), (1,)), (()...  31.3 us
    all_gather x1, waiting for transfers between devices, per_device(): lax.all_gather(value_weight, 'dp', axis=0, tiled=True)  26.6 us
    sub x1, other arithmetic, attend(): shifted = jnp.exp(scores - jnp.max(scores, axis=-1, keepdims=True))  18.1 us
    dot_general x1, matrix products, per_device(): lax.dot_general(projector, context_t, (((0,), (1,)), ((), ())), preferred...  14.8 us
    dot_general x1, matrix products, attend_back(): jnp.einsum('hgqk,khd->qhgd', scaled, key_heads[:limit], preferred_element...  14.4 us
  transfers between devices with their start and end apart: 6, of which 5 were waited for; matrix products, arithmetic and copies ran while one was open for 18% of the time, Pallas kernels for 0%

commit v1 on v0

--- a/solution.py
+++ b/solution.py
@@ -1,6 +1,10 @@
+import functools
+
 import jax
 import jax.numpy as jnp
 from jax import lax
+from jax.experimental import pallas as pl
+from jax.experimental.pallas import tpu as pltpu
 from jax.sharding import PartitionSpec as P
 
 HEAD = 128
@@ -8,6 +12,7 @@
 TKVH = 8
 SQH = 32
 SKVH = 8
+VMEM_LIMIT = 63 * 1024 * 1024
 
 
 def attend(queries, keys, values, groups, factor):
@@ -89,6 +94,506 @@
     )
 
 
+MESH = pl.DeviceIdType.MESH
+FACTOR = HEAD ** (-0.5)
+NT = (((1,), (1,)), ((), ()))
+TN = (((0,), (0,)), ((), ()))
+
+
+def dot(a, b, dims=(((1,), (0,)), ((), ()))):
+    return lax.dot_general(a, b, dims, preferred_element_type=jnp.float32)
+
+
+def lanes(start, size=HEAD):
+    return pl.ds(pl.multiple_of(start, HEAD), size)
+
+
+def fused(
+    dp_count,
+    t_count,
+    tq,
+    tk,
+    tv,
+    proj,
+    xin,
+    win,
+    out,
+    wbuf,
+    xall,
+    ctx,
+    ptile,
+    stage,
+    tgt,
+    sib,
+    from_left,
+    from_right,
+    acc,
+    qkv,
+    grads,
+    gkv,
+    loc_sem,
+    tile_sem,
+    x_send,
+    x_recv,
+    t_send,
+    t_recv,
+    wl_send,
+    wl_recv,
+    wr_send,
+    wr_recv,
+    ws_send,
+    ws_recv,
+    gs_send,
+    gs_recv,
+    gl_send,
+    gl_recv,
+    gr_send,
+    gr_recv,
+):
+    line = dp_count // 2
+    groups = win.shape[0]
+    width = win.shape[2]
+    rows = win.shape[1]
+    length = tq.shape[0]
+    share = xin.shape[0]
+    ratio = width // HEAD - 2
+    t_heads = tq.shape[1] // HEAD
+    t_ratio = t_heads // (tk.shape[1] // HEAD)
+    cols = stage.shape[2]
+    tile = ptile.shape[2]
+    dp = lax.axis_index("dp")
+    ten = lax.axis_index("tensor")
+    p = dp // 2
+    c = dp % 2
+    has_left = p > 0
+    has_right = p < line - 1
+    left = {"dp": dp - 2}
+    right = {"dp": dp + 2}
+    sibling = {"dp": dp + 1 - 2 * c}
+
+    def peer(r):
+        return {"tensor": lax.rem(ten + r, t_count)}
+
+    def remote(src, dst, send, recv, device):
+        return pltpu.make_async_remote_copy(
+            src_ref=src,
+            dst_ref=dst,
+            send_sem=send,
+            recv_sem=recv,
+            device_id=device,
+            device_id_type=MESH,
+        )
+
+    barrier = pltpu.get_barrier_semaphore()
+
+    def hello(device):
+        pl.semaphore_signal(barrier, inc=1, device_id=device, device_id_type=MESH)
+
+    @pl.when(has_left)
+    def _():
+        hello(left)
+
+    @pl.when(has_right)
+    def _():
+        hello(right)
+
+    hello(sibling)
+    for r in range(1, t_count):
+        hello(peer(r))
+    pl.semaphore_wait(
+        barrier, t_count + has_left.astype(jnp.int32) + has_right.astype(jnp.int32)
+    )
+
+    def w_left(g, s):
+        spot = wbuf.at[g, dp + 2 * s]
+        return remote(
+            win.at[g] if s == 0 else spot,
+            spot,
+            wl_send.at[g, s],
+            wl_recv.at[g, s],
+            left,
+        )
+
+    def w_right(g, s):
+        spot = wbuf.at[g, dp - 2 * s]
+        return remote(
+            win.at[g] if s == 0 else spot,
+            spot,
+            wr_send.at[g, s],
+            wr_recv.at[g, s],
+            right,
+        )
+
+    def w_sib(g, o, own=False):
+        spot = wbuf.at[g, 2 * o + c]
+        return remote(
+            win.at[g] if own else spot, spot, ws_send.at[g, o], ws_recv.at[g, o], sibling
+        )
+
+    def w_begin(g):
+        @pl.when(has_left)
+        def _():
+            w_left(g, 0).start()
+
+        @pl.when(has_right)
+        def _():
+            w_right(g, 0).start()
+
+        w_sib(g, p, True).start()
+
+    def w_step(g, s):
+        @pl.when(p >= s)
+        def _():
+            spot = wbuf.at[g, dp - 2 * s]
+            remote(spot, spot, wr_send.at[g, s], wr_recv.at[g, s - 1], right).wait_recv()
+
+            @pl.when(has_right)
+            def _():
+                w_right(g, s).start()
+
+            w_sib(g, p - s).start()
+
+        @pl.when(p + s < line)
+        def _():
+            spot = wbuf.at[g, dp + 2 * s]
+            remote(spot, spot, wl_send.at[g, s], wl_recv.at[g, s - 1], left).wait_recv()
+
+            @pl.when(has_left)
+            def _():
+                w_left(g, s).start()
+
+            w_sib(g, p + s).start()
+
+    def w_finish(g):
+        for s in range(line):
+
+            @pl.when(has_left & (p + s < line))
+            def _():
+                w_left(g, s).wait_send()
+
+            @pl.when(has_right & (p >= s))
+            def _():
+                w_right(g, s).wait_send()
+
+        for o in range(line):
+            w_sib(g, o).wait_send()
+            spot = wbuf.at[g, 2 * o + 1 - c]
+            remote(spot, spot, ws_send.at[g, o], ws_recv.at[g, o], sibling).wait_recv()
+        pltpu.make_async_copy(win.at[g], wbuf.at[g, dp], loc_sem.at[g]).wait()
+
+    def x_spot(t):
+        return xall.at[pl.ds(pl.multiple_of(t * share, 16), share)]
+
+    def x_copy(r):
+        return remote(xin, x_spot(ten), x_send.at[r - 1], x_recv.at[r - 1], peer(r))
+
+    def x_wait():
+        for r in range(1, t_count):
+            x_copy(r).wait_send()
+            spot = x_spot(lax.rem(ten + t_count - r, t_count))
+            remote(spot, spot, x_send.at[r - 1], x_recv.at[r - 1], peer(r)).wait_recv()
+        pltpu.make_async_copy(xin, x_spot(ten), loc_sem.at[groups]).wait()
+
+    def t_copy(r):
+        return remote(stage.at[r], tgt.at[r - 1], t_send.at[r - 1], t_recv.at[r - 1], peer(r))
+
+    w_begin(0)
+    for r in range(1, t_count):
+        x_copy(r).start()
+    for g in range(groups):
+        pltpu.make_async_copy(win.at[g], wbuf.at[g, dp], loc_sem.at[g]).start()
+    pltpu.make_async_copy(xin, x_spot(ten), loc_sem.at[groups]).start()
+
+    per_owner = cols // tile
+    tiles = t_count * per_owner
+
+    def tile_copy(i):
+        owner = lax.rem(ten + 1 + i // per_owner, t_count)
+        return pltpu.make_async_copy(
+            proj.at[:, lanes(owner * cols + (i % per_owner) * tile, tile)],
+            ptile.at[i % 2],
+            tile_sem.at[i % 2],
+        )
+
+    tile_copy(0).start()
+    tile_copy(1).start()
+
+    visible = lax.broadcasted_iota(jnp.int32, (length, length), 1) <= lax.broadcasted_iota(
+        jnp.int32, (length, length), 0
+    )
+
+    def weigh(q, k):
+        scores = jnp.where(visible, dot(q, k, NT) * FACTOR, -1e30)
+        shifted = jnp.exp(scores - jnp.max(scores, axis=-1, keepdims=True))
+        return shifted, jnp.sum(shifted, axis=-1, keepdims=True)
+
+    def teacher_head(h, carry):
+        kv = lanes((h // t_ratio) * HEAD)
+        shifted, total = weigh(tq[:, lanes(h * HEAD)], tk[:, kv])
+        ctx[:, lanes(h * HEAD)] = (
+            dot(shifted.astype(jnp.bfloat16), tv[:, kv]) / total
+        ).astype(jnp.bfloat16)
+        return carry
+
+    lax.fori_loop(0, t_heads // 2, teacher_head, 0)
+    w_step(0, 1)
+    lax.fori_loop(t_heads // 2, t_heads, teacher_head, 0)
+    for i in range(tiles):
+        tile_copy(i).wait()
+        r = (1 + i // per_owner) % t_count
+        stage[r, :, pl.ds((i % per_owner) * tile, tile)] = dot(ctx[...], ptile[i % 2]).astype(
+            jnp.bfloat16
+        )
+        if i + 2 < tiles:
+            tile_copy(i + 2).start()
+        if r and i % per_owner == per_owner - 1:
+            t_copy(r).start()
+        if i == tiles // 4:
+            for s in range(2, line - 1):
+                w_step(0, s)
+            if groups > 1:
+                w_begin(1)
+    if line > 2:
+        w_step(0, line - 1)
+    x_wait()
+
+    def x_cols(d):
+        return xall[:, lanes(d * rows, rows)]
+
+    def project(g):
+        acc[...] = dot(x_cols(0), wbuf[g, 0])
+
+        def one(d, carry):
+            acc[...] += dot(x_cols(d), wbuf[g, d])
+            return carry
+
+        lax.fori_loop(1, dp_count, one, 0)
+        qkv[...] = acc[...].astype(jnp.bfloat16)
+
+    def heads(g, first, last):
+        def one(j, carry):
+            q = qkv[:, lanes(j * HEAD)]
+            k = qkv[:, pl.ds(ratio * HEAD, HEAD)]
+            v = qkv[:, pl.ds((ratio + 1) * HEAD, HEAD)]
+            shifted, total = weigh(q, k)
+            probs = shifted / total
+            rounded = probs.astype(jnp.bfloat16)
+            spot = lanes((g * ratio + j) * HEAD)
+            target = stage[0, :, spot].astype(jnp.float32)
+            for r in range(t_count - 1):
+                target += tgt[r, :, spot].astype(jnp.float32)
+            incoming = ((dot(rounded, v) - target) / dp_count).astype(jnp.bfloat16)
+            gkv[1] += dot(rounded, incoming, TN)
+            grad = dot(incoming, v, NT)
+            grad = probs * (grad - jnp.sum(grad * probs, axis=-1, keepdims=True))
+            scaled = (grad * FACTOR).astype(jnp.bfloat16)
+            grads[:, lanes(j * HEAD)] = dot(scaled, k).astype(jnp.bfloat16)
+            gkv[0] += dot(scaled, q, TN)
+            return carry
+
+        lax.fori_loop(first, last, one, 0)
+
+    def g_sib(g, o):
+        return remote(
+            wbuf.at[g, 2 * o + 1 - c], sib.at[g, o], gs_send.at[g, o], gs_recv.at[g, o], sibling
+        )
+
+    def g_right(g, k):
+        o = line - 1 - k
+        slot = o - p - 1
+        return remote(
+            wbuf.at[g, 2 * o + c],
+            from_left.at[g, slot],
+            gr_send.at[g, k],
+            gr_recv.at[g, slot],
+            right,
+        )
+
+    def g_left(g, k):
+        slot = p - 1 - k
+        return remote(
+            wbuf.at[g, 2 * k + c],
+            from_right.at[g, slot],
+            gl_send.at[g, k],
+            gl_recv.at[g, slot],
+            left,
+        )
+
+    def wait_left(g, slot):
+        spot = from_left.at[g, slot]
+        remote(spot, spot, gr_send.at[g, 0], gr_recv.at[g, slot], right).wait_recv()
+
+    def wait_right(g, slot):
+        spot = from_right.at[g, slot]
+        remote(spot, spot, gl_send.at[g, 0], gl_recv.at[g, slot], left).wait_recv()
+
+    def products(g):
+        for j in range(2):
+            grads[:, pl.ds((ratio + j) * HEAD, HEAD)] = gkv[j].astype(jnp.bfloat16)
+
+        def one(i, carry):
+            o = jnp.where(i % 2 == 0, i // 2, line - 1 - i // 2)
+            d = 2 * o + 1 - c
+            wbuf[g, d] = dot(x_cols(d), grads[...], TN).astype(jnp.bfloat16)
+            g_sib(g, o).start()
+            d = 2 * o + c
+            wbuf[g, d] = dot(x_cols(d), grads[...], TN).astype(jnp.bfloat16)
+            return carry
+
+        lax.fori_loop(0, line, one, 0)
+
+    def pair(g, o):
+        g_sib(g, o).wait_recv()
+        return wbuf[g, 2 * o + c].astype(jnp.float32) + sib[g, o].astype(jnp.float32)
+
+    def g_step(g, k):
+        o = line - 1 - k
+
+        @pl.when(o > p)
+        def _():
+            wbuf[g, 2 * o + c] = pair(g, o).astype(jnp.bfloat16)
+
+            @pl.when(has_left)
+            def _():
+                wait_left(g, o - p)
+                wbuf[g, 2 * o + c] = (
+                    wbuf[g, 2 * o + c].astype(jnp.float32)
+                    + from_left[g, o - p].astype(jnp.float32)
+                ).astype(jnp.bfloat16)
+
+            g_right(g, k).start()
+
+        @pl.when(k < p)
+        def _():
+            wbuf[g, 2 * k + c] = pair(g, k).astype(jnp.bfloat16)
+
+            @pl.when(has_right)
+            def _():
+                wait_right(g, p - k)
+                wbuf[g, 2 * k + c] = (
+                    wbuf[g, 2 * k + c].astype(jnp.float32)
+                    + from_right[g, p - k].astype(jnp.float32)
+                ).astype(jnp.bfloat16)
+
+            g_left(g, k).start()
+
+    def g_finish(g):
+        out[g] = pair(g, p)
+
+        @pl.when(has_left)
+        def _():
+            wait_left(g, 0)
+            out[g] += from_left[g, 0].astype(jnp.float32)
+
+        @pl.when(has_right)
+        def _():
+            wait_right(g, 0)
+            out[g] += from_right[g, 0].astype(jnp.float32)
+
+        for k in range(line - 1):
+
+            @pl.when(line - 1 - k > p)
+            def _():
+                g_right(g, k).wait_send()
+
+            @pl.when(k < p)
+            def _():
+                g_left(g, k).wait_send()
+
+        for o in range(line):
+            g_sib(g, o).wait_send()
+
+    for g in range(groups):
+        work = []
+        if g:
+            work += [functools.partial(g_step, g - 1, k) for k in range(line - 1)]
+            work += [functools.partial(g_finish, g - 1)]
+        if g + 1 < groups:
+            work += [functools.partial(w_step, g + 1, s) for s in range(1, line)]
+        if g > 0 and g + 1 < groups:
+            w_begin(g + 1)
+        w_finish(g)
+        if g and work:
+            work.pop(0)()
+        project(g)
+        if g == 0:
+            for r in range(1, t_count):
+                t_copy(r).wait()
+        gkv[...] = jnp.zeros_like(gkv)
+        for j in range(ratio):
+            if work:
+                work.pop(0)()
+            heads(g, j, j + 1)
+        while work:
+            work.pop(0)()
+        products(g)
+    for k in range(line - 1):
+        g_step(groups - 1, k)
+    g_finish(groups - 1)
+
+
+def fused_call(tq, tk, tv, projector, xin, query_weight, key_weight, value_weight):
+    dp_count = lax.axis_size("dp")
+    t_count = lax.axis_size("tensor")
+    line = dp_count // 2
+    groups = key_weight.shape[1] // HEAD
+    rows = query_weight.shape[0]
+    q_cols = query_weight.shape[1]
+    per = q_cols // groups
+    width = per + 2 * HEAD
+    length = tq.shape[0]
+    win = jnp.concatenate(
+        [
+            query_weight.reshape(rows, groups, per),
+            key_weight.reshape(rows, groups, HEAD),
+            value_weight.reshape(rows, groups, HEAD),
+        ],
+        axis=2,
+    ).transpose(1, 0, 2)
+    cols = projector.shape[1] // t_count
+    tile = min(512, cols)
+    bf = jnp.bfloat16
+    vmem = pl.BlockSpec(memory_space=pltpu.VMEM)
+    hbm = pl.BlockSpec(memory_space=pl.ANY)
+    sem = pltpu.SemaphoreType.DMA
+    out = pl.pallas_call(
+        functools.partial(fused, dp_count, t_count),
+        out_shape=jax.ShapeDtypeStruct((groups, rows, width), jnp.float32),
+        in_specs=[vmem, vmem, vmem, hbm, hbm, hbm],
+        out_specs=vmem,
+        scratch_shapes=[
+            pltpu.VMEM((groups, dp_count, rows, width), bf),
+            pltpu.VMEM((length, xin.shape[1]), bf),
+            pltpu.VMEM(tq.shape, bf),
+            pltpu.VMEM((2, projector.shape[0], tile), bf),
+            pltpu.VMEM((t_count, length, cols), bf),
+            pltpu.VMEM((t_count - 1, length, cols), bf),
+            pltpu.VMEM((groups, line, rows, width), bf),
+            pltpu.VMEM((groups, line - 1, rows, width), bf),
+            pltpu.VMEM((groups, line - 1, rows, width), bf),
+            pltpu.VMEM((length, width), jnp.float32),
+            pltpu.VMEM((length, width), bf),
+            pltpu.VMEM((length, width), bf),
+            pltpu.VMEM((2, length, HEAD), jnp.float32),
+            sem((groups + 1,)),
+            sem((2,)),
+            sem((t_count - 1,)),
+            sem((t_count - 1,)),
+            sem((t_count - 1,)),
+            sem((t_count - 1,)),
+        ]
+        + [sem((groups, line))] * 12,
+        compiler_params=pltpu.CompilerParams(
+            collective_id=0, has_side_effects=True, vmem_limit_bytes=VMEM_LIMIT
+        ),
+    )(tq, tk, tv, projector, xin, win)
+    return (
+        jnp.concatenate([out[g, :, :per] for g in range(groups)], axis=1),
+        jnp.concatenate([out[g, :, per : per + HEAD] for g in range(groups)], axis=1),
+        jnp.concatenate([out[g, :, per + HEAD :] for g in range(groups)], axis=1),
+    )
+
+
 def per_device(
     teacher_queries,
     teacher_keys,
@@ -99,6 +604,17 @@
     key_weight,
     value_weight,
 ):
+    if teacher_queries.shape[1] <= 512:
+        return fused_call(
+            teacher_queries[0],
+            teacher_keys[0],
+            teacher_values[0],
+            projector,
+            student_inputs[0],
+            query_weight,
+            key_weight,
+            value_weight,
+        )
     factor = HEAD ** (-0.5)
     dp_count = lax.axis_size("dp")
     context_t, unused = attend(

time: 456 us -> 295 us (0.65)
  waiting for transfers between devices: 301 us -> 0 us
  Pallas kernels: 0 us -> 285 us
  matrix products: 106 us -> 0 us
  other arithmetic: 19.8 us -> 3.83 us
  between operations: 14.3 us -> 0.73 us
  local copies, waits for them, and re-layouts: 13.8 us -> 4.5 us
    pallas_call x0 -> x1, Pallas kernels: none -> 285 us  [fused_call(): pl.pallas_call(functools.partial(fused, dp_count, t_count), out_shape=jax...]
    reduce_scatter x2 -> x0, waiting for transfers between devices: 161 us -> none  [the longest x1 129 us: per_device(): lax.psum_scatter(whole.astype(jnp.bfloat16), 'dp', scatter_dimension=0, t...]
    all_gather x4 -> x0, waiting for transfers between devices: 138 us -> none  [the longest x1 78.9 us: per_device(): lax.all_gather(query_weight, 'dp', axis=0, tiled=True)]
    dot_general x12 -> x0, matrix products: 101 us -> none  [the longest x1 14.8 us: per_device(): lax.dot_general(projector, context_t, (((0,), (1,)), ((), ())), preferred...]
    sub x1 -> x0, other arithmetic: 18.1 us -> none  [attend(): shifted = jnp.exp(scores - jnp.max(scores, axis=-1, keepdims=True))]
    sub x1 -> x0, matrix products: 5.39 us -> none  [attend(): shifted = jnp.exp(scores - jnp.max(scores, axis=-1, keepdims=True))]
  transfers between devices with their start and end apart: 6 -> 0, of which waited for: 5 -> 0; matrix products, arithmetic and copies ran while one was open for 18% -> 0% of each run, Pallas kernels for 0% -> 0%
where the time goes in v1:
time: 295 us; the launch traced here: 294 us
  Pallas kernels  285 us (97%)
  local copies, waits for them, and re-layouts  4.5 us (2%)
  other arithmetic  3.83 us (1%)
    pallas_call x1, Pallas kernels, fused_call(): pl.pallas_call(functools.partial(fused, dp_count, t_count), out_shape=jax...  285 us

profile of v1, /device:TPU:0, one launch (start us, length us, event | category | flops | bytes accessed | tf_op | source)
XLA Modules:
  0.0 294.4 jit_solution(6298219896113822489)
XLA Ops:
  0.6 0.0 copy-start.1
  0.6 1.5 copy.11
  2.2 0.0 copy-start.2
  2.2 0.5 copy.14
  2.8 0.0 copy-done.1
  2.8 0.1 copy.12
  2.9 0.2 copy.15
  3.1 0.1 copy-done.2
  3.1 0.1 copy.13
  3.3 0.2 copy.16
  3.5 1.3 maximum_bitcast_fusion.win
  4.7 285.3 %shard_map.103 = f32[2,512,768]{2,1,0:T(8,128)} custom-call(bf16[512,2048]{1,0:T(8,128)(2,1)} %bitcast.22, bf16[512,256]{1,0:T(8,128)(2,1)} %bitcast.26, bf16[512,256]{1,0:T(8,128)(2,1)} %bitcast.27, bf16[2048,4096]{1,0:T(8,128)(2,1)} %proj.1, bf16[128,4096]{1,0:T(8,128)(2,1)} %bitcast.23, bf16[2,512,768]{2,1,0:T(8,128)(2,1)} %maximum_bitcast_fusion.win), custom_call_target="tpu_custom_call" | custom-call | tf_op jit(solution)/shard_map/pallas_call | solution.py:559
  290.1 0.0 copy-start
  290.1 1.4 slice_bitcast_fusion.3
  291.5 1.0 pad_maximum_fusion.1
  292.6 0.0 copy-done
  292.6 0.3 slice_bitcast_fusion.1
  292.9 1.5 pad_maximum_fusion
Async XLA Ops:
  0.6 2.1 copy-start.1
  2.2 1.0 copy-start.2
  290.1 2.5 copy-start

commit v2 on v1

--- a/solution.py
+++ b/solution.py
@@ -160,7 +160,7 @@
     t_heads = tq.shape[1] // HEAD
     t_ratio = t_heads // (tk.shape[1] // HEAD)
     cols = stage.shape[2]
-    tile = ptile.shape[2]
+    tile = ratio * HEAD
     dp = lax.axis_index("dp")
     ten = lax.axis_index("tensor")
     p = dp // 2
@@ -294,8 +294,15 @@
             remote(spot, spot, x_send.at[r - 1], x_recv.at[r - 1], peer(r)).wait_recv()
         pltpu.make_async_copy(xin, x_spot(ten), loc_sem.at[groups]).wait()
 
-    def t_copy(r):
-        return remote(stage.at[r], tgt.at[r - 1], t_send.at[r - 1], t_recv.at[r - 1], peer(r))
+    def t_copy(r, part):
+        spot = pl.ds(part * tile, tile)
+        return remote(
+            stage.at[r, :, spot],
+            tgt.at[r - 1, :, spot],
+            t_send.at[r - 1, part],
+            t_recv.at[r - 1, part],
+            peer(r),
+        )
 
     w_begin(0)
     for r in range(1, t_count):
@@ -304,61 +311,78 @@
         pltpu.make_async_copy(win.at[g], wbuf.at[g, dp], loc_sem.at[g]).start()
     pltpu.make_async_copy(xin, x_spot(ten), loc_sem.at[groups]).start()
 
-    per_owner = cols // tile
-    tiles = t_count * per_owner
+    tiles = t_count * (cols // tile)
+    deep = proj.shape[0]
+
+    def tile_spot(i):
+        return pl.ds((i % 2) * deep, deep), pl.ds(0, tile)
 
     def tile_copy(i):
-        owner = lax.rem(ten + 1 + i // per_owner, t_count)
+        owner = lax.rem(ten + 1 + i % t_count, t_count)
         return pltpu.make_async_copy(
-            proj.at[:, lanes(owner * cols + (i % per_owner) * tile, tile)],
-            ptile.at[i % 2],
+            proj.at[:, lanes(owner * cols + (i // t_count) * tile, tile)],
+            ptile.at[tile_spot(i)],
             tile_sem.at[i % 2],
         )
 
     tile_copy(0).start()
     tile_copy(1).start()
 
-    visible = lax.broadcasted_iota(jnp.int32, (length, length), 1) <= lax.broadcasted_iota(
-        jnp.int32, (length, length), 0
-    )
-
-    def weigh(q, k):
+    def weigh(q, k, first):
+        shape = (q.shape[0], k.shape[0])
+        visible = lax.broadcasted_iota(jnp.int32, shape, 1) <= first + lax.broadcasted_iota(
+            jnp.int32, shape, 0
+        )
         scores = jnp.where(visible, dot(q, k, NT) * FACTOR, -1e30)
         shifted = jnp.exp(scores - jnp.max(scores, axis=-1, keepdims=True))
-        return shifted, jnp.sum(shifted, axis=-1, keepdims=True)
+        return shifted, 1.0 / jnp.sum(shifted, axis=-1, keepdims=True)
+
+    half = length // 2 if length % 512 == 0 else length
+    blocks = [(first, first + half) for first in range(0, length, half)]
 
     def teacher_head(h, carry):
         kv = lanes((h // t_ratio) * HEAD)
-        shifted, total = weigh(tq[:, lanes(h * HEAD)], tk[:, kv])
-        ctx[:, lanes(h * HEAD)] = (
-            dot(shifted.astype(jnp.bfloat16), tv[:, kv]) / total
-        ).astype(jnp.bfloat16)
+        spot = lanes(h * HEAD)
+        for first, limit in blocks:
+            shifted, inverse = weigh(tq[first:limit, spot], tk[:limit, kv], first)
+            ctx[first:limit, spot] = (
+                dot(shifted.astype(jnp.bfloat16), tv[:limit, kv]) * inverse
+            ).astype(jnp.bfloat16)
         return carry
 
-    lax.fori_loop(0, t_heads // 2, teacher_head, 0)
+    lax.fori_loop(0, 3 * t_heads // 4, teacher_head, 0)
     w_step(0, 1)
-    lax.fori_loop(t_heads // 2, t_heads, teacher_head, 0)
+    lax.fori_loop(3 * t_heads // 4, t_heads, teacher_head, 0)
     for i in range(tiles):
         tile_copy(i).wait()
-        r = (1 + i // per_owner) % t_count
-        stage[r, :, pl.ds((i % per_owner) * tile, tile)] = dot(ctx[...], ptile[i % 2]).astype(
+        r = (1 + i) % t_count
+        part = i // t_count
+        stage[r, :, pl.ds(part * tile, tile)] = dot(ctx[...], ptile[tile_spot(i)]).astype(
             jnp.bfloat16
         )
         if i + 2 < tiles:
             tile_copy(i + 2).start()
-        if r and i % per_owner == per_owner - 1:
-            t_copy(r).start()
-        if i == tiles // 4:
-            for s in range(2, line - 1):
-                w_step(0, s)
-            if groups > 1:
-                w_begin(1)
+        if r:
+            t_copy(r, part).start()
+    for s in range(2, line - 1):
+        w_step(0, s)
+    if groups > 1:
+        w_begin(1)
+    x_wait()
+
+    def x_turned(d):
+        return ptile[pl.ds(pl.multiple_of(d * rows, rows), rows), pl.ds(0, length)]
+
+    def turn(d, carry):
+        ptile[pl.ds(pl.multiple_of(d * rows, rows), rows), pl.ds(0, length)] = x_cols(d).T
+        return carry
+
+    def x_cols(d):
+        return xall[:, lanes(d * rows, rows)]
+
+    lax.fori_loop(0, dp_count, turn, 0)
     if line > 2:
         w_step(0, line - 1)
-    x_wait()
-
-    def x_cols(d):
-        return xall[:, lanes(d * rows, rows)]
 
     def project(g):
         acc[...] = dot(x_cols(0), wbuf[g, 0])
@@ -370,166 +394,198 @@
         lax.fori_loop(1, dp_count, one, 0)
         qkv[...] = acc[...].astype(jnp.bfloat16)
 
-    def heads(g, first, last):
+    def heads(g, begin, end):
         def one(j, carry):
-            q = qkv[:, lanes(j * HEAD)]
-            k = qkv[:, pl.ds(ratio * HEAD, HEAD)]
-            v = qkv[:, pl.ds((ratio + 1) * HEAD, HEAD)]
-            shifted, total = weigh(q, k)
-            probs = shifted / total
-            rounded = probs.astype(jnp.bfloat16)
+            lane = lanes(j * HEAD)
             spot = lanes((g * ratio + j) * HEAD)
-            target = stage[0, :, spot].astype(jnp.float32)
-            for r in range(t_count - 1):
-                target += tgt[r, :, spot].astype(jnp.float32)
-            incoming = ((dot(rounded, v) - target) / dp_count).astype(jnp.bfloat16)
-            gkv[1] += dot(rounded, incoming, TN)
-            grad = dot(incoming, v, NT)
-            grad = probs * (grad - jnp.sum(grad * probs, axis=-1, keepdims=True))
-            scaled = (grad * FACTOR).astype(jnp.bfloat16)
-            grads[:, lanes(j * HEAD)] = dot(scaled, k).astype(jnp.bfloat16)
-            gkv[0] += dot(scaled, q, TN)
+            for first, limit in blocks:
+                q = qkv[first:limit, lane]
+                k = qkv[:limit, pl.ds(ratio * HEAD, HEAD)]
+                v = qkv[:limit, pl.ds((ratio + 1) * HEAD, HEAD)]
+                shifted, inverse = weigh(q, k, first)
+                probs = shifted * inverse
+                rounded = probs.astype(jnp.bfloat16)
+                target = stage[0, first:limit, spot].astype(jnp.float32)
+                for r in range(t_count - 1):
+                    target += tgt[r, first:limit, spot].astype(jnp.float32)
+                incoming = ((dot(rounded, v) - target) / dp_count).astype(jnp.bfloat16)
+                gkv[1, :limit] += dot(rounded, incoming, TN)
+                grad = dot(incoming, v, NT)
+                grad = probs * (grad - jnp.sum(grad * probs, axis=-1, keepdims=True))
+                scaled = (grad * FACTOR).astype(jnp.bfloat16)
+                grads[first:limit, lane] = dot(scaled, k).astype(jnp.bfloat16)
+                gkv[0, :limit] += dot(scaled, q, TN)
             return carry
 
-        lax.fori_loop(first, last, one, 0)
-
-    def g_sib(g, o):
+        lax.fori_loop(begin, end, one, 0)
+
+    early = ratio - 1
+
+    def cut(ref, q, i):
+        spot = pl.ds(0, early * HEAD) if q % 2 == 0 else pl.ds(early * HEAD, 3 * HEAD)
+        return ref.at[q // 2, i, :, spot]
+
+    def g_sib(q, o):
         return remote(
-            wbuf.at[g, 2 * o + 1 - c], sib.at[g, o], gs_send.at[g, o], gs_recv.at[g, o], sibling
-        )
-
-    def g_right(g, k):
+            cut(wbuf, q, 2 * o + 1 - c),
+            cut(sib, q, o),
+            gs_send.at[q, o],
+            gs_recv.at[q, o],
+            sibling,
+        )
+
+    def g_right(q, k):
         o = line - 1 - k
         slot = o - p - 1
         return remote(
-            wbuf.at[g, 2 * o + c],
-            from_left.at[g, slot],
-            gr_send.at[g, k],
-            gr_recv.at[g, slot],
+            cut(wbuf, q, 2 * o + c),
+            cut(from_left, q, slot),
+            gr_send.at[q, k],
+            gr_recv.at[q, slot],
             right,
         )
 
-    def g_left(g, k):
+    def g_left(q, k):
         slot = p - 1 - k
         return remote(
-            wbuf.at[g, 2 * k + c],
-            from_right.at[g, slot],
-            gl_send.at[g, k],
-            gl_recv.at[g, slot],
+            cut(wbuf, q, 2 * k + c),
+            cut(from_right, q, slot),
+            gl_send.at[q, k],
+            gl_recv.at[q, slot],
             left,
         )
 
-    def wait_left(g, slot):
-        spot = from_left.at[g, slot]
-        remote(spot, spot, gr_send.at[g, 0], gr_recv.at[g, slot], right).wait_recv()
-
-    def wait_right(g, slot):
-        spot = from_right.at[g, slot]
-        remote(spot, spot, gl_send.at[g, 0], gl_recv.at[g, slot], left).wait_recv()
-
-    def products(g):
-        for j in range(2):
-            grads[:, pl.ds((ratio + j) * HEAD, HEAD)] = gkv[j].astype(jnp.bfloat16)
+    def wait_left(q, slot):
+        spot = cut(from_left, q, slot)
+        remote(spot, spot, gr_send.at[q, 0], gr_recv.at[q, slot], right).wait_recv()
+        return spot[...].astype(jnp.float32)
+
+    def wait_right(q, slot):
+        spot = cut(from_right, q, slot)
+        remote(spot, spot, gl_send.at[q, 0], gl_recv.at[q, slot], left).wait_recv()
+        return spot[...].astype(jnp.float32)
+
+    def pair(q, o):
+        g_sib(q, o).wait_recv()
+        return cut(wbuf, q, 2 * o + c)[...].astype(jnp.float32) + cut(sib, q, o)[...].astype(
+            jnp.float32
+        )
+
+    def products(q):
+        if q % 2:
+            for j in range(2):
+                grads[:, pl.ds((ratio + j) * HEAD, HEAD)] = gkv[j].astype(jnp.bfloat16)
+            spot = pl.ds(early * HEAD, 3 * HEAD)
+        else:
+            spot = pl.ds(0, early * HEAD)
 
         def one(i, carry):
-            o = jnp.where(i % 2 == 0, i // 2, line - 1 - i // 2)
-            d = 2 * o + 1 - c
-            wbuf[g, d] = dot(x_cols(d), grads[...], TN).astype(jnp.bfloat16)
-            g_sib(g, o).start()
-            d = 2 * o + c
-            wbuf[g, d] = dot(x_cols(d), grads[...], TN).astype(jnp.bfloat16)
+            o = jnp.where(i % 2 == 0, line - 1 - i // 2, i // 2)
+            for core in (1 - c, c):
+                d = 2 * o + core
+                wbuf[q // 2, d, :, spot] = dot(x_turned(d), grads[:, spot]).astype(jnp.bfloat16)
+                if core is not c:
+                    g_sib(q, o).start()
             return carry
 
         lax.fori_loop(0, line, one, 0)
 
-    def pair(g, o):
-        g_sib(g, o).wait_recv()
-        return wbuf[g, 2 * o + c].astype(jnp.float32) + sib[g, o].astype(jnp.float32)
-
-    def g_step(g, k):
+        @pl.when(p == 0)
+        def _():
+            for k in range(line - 1):
+                spot = cut(wbuf, q, 2 * (line - 1 - k) + c)
+                spot[...] = pair(q, line - 1 - k).astype(jnp.bfloat16)
+                g_right(q, k).start()
+
+        @pl.when(p == line - 1)
+        def _():
+            for k in range(line - 1):
+                spot = cut(wbuf, q, 2 * k + c)
+                spot[...] = pair(q, k).astype(jnp.bfloat16)
+                g_left(q, k).start()
+
+    def chain(q, k):
         o = line - 1 - k
 
-        @pl.when(o > p)
-        def _():
-            wbuf[g, 2 * o + c] = pair(g, o).astype(jnp.bfloat16)
-
-            @pl.when(has_left)
-            def _():
-                wait_left(g, o - p)
-                wbuf[g, 2 * o + c] = (
-                    wbuf[g, 2 * o + c].astype(jnp.float32)
-                    + from_left[g, o - p].astype(jnp.float32)
-                ).astype(jnp.bfloat16)
-
-            g_right(g, k).start()
-
-        @pl.when(k < p)
-        def _():
-            wbuf[g, 2 * k + c] = pair(g, k).astype(jnp.bfloat16)
-
-            @pl.when(has_right)
-            def _():
-                wait_right(g, p - k)
-                wbuf[g, 2 * k + c] = (
-                    wbuf[g, 2 * k + c].astype(jnp.float32)
-                    + from_right[g, p - k].astype(jnp.float32)
-                ).astype(jnp.bfloat16)
-
-            g_left(g, k).start()
-
-    def g_finish(g):
-        out[g] = pair(g, p)
+        @pl.when(has_left & (o > p))
+        def _():
+            own = pair(q, o)
+            spot = cut(wbuf, q, 2 * o + c)
+            spot[...] = (own + wait_left(q, o - p)).astype(jnp.bfloat16)
+            g_right(q, k).start()
+
+        @pl.when(has_right & (k < p))
+        def _():
+            own = pair(q, k)
+            spot = cut(wbuf, q, 2 * k + c)
+            spot[...] = (own + wait_right(q, p - k)).astype(jnp.bfloat16)
+            g_left(q, k).start()
+
+    def finish(q):
+        spot = pl.ds(0, early * HEAD) if q % 2 == 0 else pl.ds(early * HEAD, 3 * HEAD)
+        total = out.at[q // 2, :, spot]
+        total[...] = pair(q, p)
 
         @pl.when(has_left)
         def _():
-            wait_left(g, 0)
-            out[g] += from_left[g, 0].astype(jnp.float32)
+            total[...] += wait_left(q, 0)
 
         @pl.when(has_right)
         def _():
-            wait_right(g, 0)
-            out[g] += from_right[g, 0].astype(jnp.float32)
+            total[...] += wait_right(q, 0)
 
         for k in range(line - 1):
 
             @pl.when(line - 1 - k > p)
             def _():
-                g_right(g, k).wait_send()
+                g_right(q, k).wait_send()
 
             @pl.when(k < p)
             def _():
-                g_left(g, k).wait_send()
+                g_left(q, k).wait_send()
 
         for o in range(line):
-            g_sib(g, o).wait_send()
-
+            g_sib(q, o).wait_send()
+
+    links = range(line - 2)
     for g in range(groups):
         work = []
         if g:
-            work += [functools.partial(g_step, g - 1, k) for k in range(line - 1)]
-            work += [functools.partial(g_finish, g - 1)]
+            for q in (2 * g - 2, 2 * g - 1):
+                work += [functools.partial(chain, q, k) for k in links]
+            work += [functools.partial(finish, 2 * g - 2), functools.partial(finish, 2 * g - 1)]
+        ahead = []
         if g + 1 < groups:
-            work += [functools.partial(w_step, g + 1, s) for s in range(1, line)]
-        if g > 0 and g + 1 < groups:
-            w_begin(g + 1)
+            ahead = [functools.partial(w_step, g + 1, s) for s in range(1, line)]
+            if g > 0:
+                w_begin(g + 1)
         w_finish(g)
-        if g and work:
+        if work:
             work.pop(0)()
         project(g)
-        if g == 0:
-            for r in range(1, t_count):
-                t_copy(r).wait()
         gkv[...] = jnp.zeros_like(gkv)
+        for part in range(cols // tile):
+            if (part * tile) // (ratio * HEAD) == g:
+                for r in range(1, t_count):
+                    t_copy(r, part).wait()
         for j in range(ratio):
             if work:
                 work.pop(0)()
+            if ahead and j % 2 == 0 and len(ahead) > 1:
+                ahead.pop(0)()
             heads(g, j, j + 1)
+            if j == early - 1:
+                products(2 * g)
+        products(2 * g + 1)
         while work:
             work.pop(0)()
-        products(g)
-    for k in range(line - 1):
-        g_step(groups - 1, k)
-    g_finish(groups - 1)
+        while ahead:
+            ahead.pop(0)()
+    for q in (2 * groups - 2, 2 * groups - 1):
+        for k in links:
+            chain(q, k)
+    for q in (2 * groups - 2, 2 * groups - 1):
+        finish(q)
 
 
 def fused_call(tq, tk, tv, projector, xin, query_weight, key_weight, value_weight):
@@ -551,7 +607,7 @@
         axis=2,
     ).transpose(1, 0, 2)
     cols = projector.shape[1] // t_count
-    tile = min(512, cols)
+    tile = min(per, cols)
     bf = jnp.bfloat16
     vmem = pl.BlockSpec(memory_space=pltpu.VMEM)
     hbm = pl.BlockSpec(memory_space=pl.ANY)
@@ -565,7 +621,7 @@
             pltpu.VMEM((groups, dp_count, rows, width), bf),
             pltpu.VMEM((length, xin.shape[1]), bf),
             pltpu.VMEM(tq.shape, bf),
-            pltpu.VMEM((2, projector.shape[0], tile), bf),
+            pltpu.VMEM((max(2 * projector.shape[0], xin.shape[1]), max(tile, length)), bf),
             pltpu.VMEM((t_count, length, cols), bf),
             pltpu.VMEM((t_count - 1, length, cols), bf),
             pltpu.VMEM((groups, line, rows, width), bf),
@@ -579,10 +635,11 @@
             sem((2,)),
             sem((t_count - 1,)),
             sem((t_count - 1,)),
-            sem((t_count - 1,)),
-            sem((t_count - 1,)),
+            sem((t_count - 1, cols // tile)),
+            sem((t_count - 1, cols // tile)),
         ]
-        + [sem((groups, line))] * 12,
+        + [sem((groups, line))] * 6
+        + [sem((2 * groups, line))] * 6,
         compiler_params=pltpu.CompilerParams(
             collective_id=0, has_side_effects=True, vmem_limit_bytes=VMEM_LIMIT
         ),

time: 295 us -> 228 us (0.77)
  Pallas kernels: 285 us -> 218 us
    pallas_call x1, Pallas kernels: 285 us -> 218 us  [fused_call(): pl.pallas_call(functools.partial(fused, dp_count, t_count), out_shape=jax...]
where the time goes in v2:
time: 228 us; the launch traced here: 227 us
  Pallas kernels  218 us (96%)
  local copies, waits for them, and re-layouts  4.5 us (2%)
  other arithmetic  3.83 us (2%)
    pallas_call x1, Pallas kernels, fused_call(): pl.pallas_call(functools.partial(fused, dp_count, t_count), out_shape=jax...  218 us

profile of v2, /device:TPU:0, one launch (start us, length us, event | category | flops | bytes accessed | tf_op | source)
XLA Modules:
  0.0 227.3 jit_solution(12552863454436472160)
XLA Ops:
  0.6 0.0 copy-start.1
  0.6 1.5 copy.11
  2.2 0.0 copy-start.2
  2.2 0.5 copy.14
  2.8 0.0 copy-done.1
  2.8 0.1 copy.12
  2.9 0.2 copy.15
  3.1 0.1 copy-done.2
  3.1 0.1 copy.13
  3.3 0.2 copy.16
  3.5 1.3 maximum_bitcast_fusion.win
  4.7 218.3 %shard_map.103 = f32[2,512,768]{2,1,0:T(8,128)} custom-call(bf16[512,2048]{1,0:T(8,128)(2,1)} %bitcast.22, bf16[512,256]{1,0:T(8,128)(2,1)} %bitcast.26, bf16[512,256]{1,0:T(8,128)(2,1)} %bitcast.27, bf16[2048,4096]{1,0:T(8,128)(2,1)} %proj.1, bf16[128,4096]{1,0:T(8,128)(2,1)} %bitcast.23, bf16[2,512,768]{2,1,0:T(8,128)(2,1)} %maximum_bitcast_fusion.win), custom_call_target="tpu_custom_call" | custom-call | tf_op jit(solution)/shard_map/pallas_call | solution.py:615
  223.0 0.0 copy-start
  223.0 1.4 slice_bitcast_fusion.3
  224.5 1.0 pad_maximum_fusion.1
  225.5 0.0 copy-done
  225.5 0.3 slice_bitcast_fusion.1
  225.8 1.5 pad_maximum_fusion
Async XLA Ops:
  0.6 2.1 copy-start.1
  2.2 1.0 copy-start.2
  223.0 2.5 %copy-start = (f32[2,512,768]{2,1,0:T(8,128)S(1)}, f32[2,512,768]{2,1,0:T(8,128)}, u32[]{:S(2)}) copy-start(f32[2,512,768]{2,1,0:T(8,128)} %shard_map.103) | copy-start | bytes 9437188

commit v3 on v2

--- a/solution.py
+++ b/solution.py
@@ -116,7 +116,9 @@
     tv,
     proj,
     xin,
-    win,
+    qw,
+    kw,
+    vw,
     out,
     wbuf,
     xall,
@@ -151,9 +153,9 @@
     gr_recv,
 ):
     line = dp_count // 2
-    groups = win.shape[0]
-    width = win.shape[2]
-    rows = win.shape[1]
+    groups = wbuf.shape[0]
+    width = wbuf.shape[3]
+    rows = wbuf.shape[2]
     length = tq.shape[0]
     share = xin.shape[0]
     ratio = width // HEAD - 2
@@ -184,6 +186,27 @@
             device_id_type=MESH,
         )
 
+    def own_copies(g):
+        per = ratio * HEAD
+        mine = wbuf.at[g, dp]
+        return (
+            pltpu.make_async_copy(
+                qw.at[:, pl.ds(g * per, per)], mine.at[:, pl.ds(0, per)], loc_sem.at[g, 0]
+            ),
+            pltpu.make_async_copy(
+                kw.at[:, pl.ds(g * HEAD, HEAD)], mine.at[:, pl.ds(per, HEAD)], loc_sem.at[g, 1]
+            ),
+            pltpu.make_async_copy(
+                vw.at[:, pl.ds(g * HEAD, HEAD)],
+                mine.at[:, pl.ds(per + HEAD, HEAD)],
+                loc_sem.at[g, 2],
+            ),
+        )
+
+    for g in range(groups):
+        for copy in own_copies(g):
+            copy.start()
+
     barrier = pltpu.get_barrier_semaphore()
 
     def hello(device):
@@ -207,7 +230,7 @@
     def w_left(g, s):
         spot = wbuf.at[g, dp + 2 * s]
         return remote(
-            win.at[g] if s == 0 else spot,
+            spot,
             spot,
             wl_send.at[g, s],
             wl_recv.at[g, s],
@@ -217,18 +240,16 @@
     def w_right(g, s):
         spot = wbuf.at[g, dp - 2 * s]
         return remote(
-            win.at[g] if s == 0 else spot,
+            spot,
             spot,
             wr_send.at[g, s],
             wr_recv.at[g, s],
             right,
         )
 
-    def w_sib(g, o, own=False):
+    def w_sib(g, o):
         spot = wbuf.at[g, 2 * o + c]
-        return remote(
-            win.at[g] if own else spot, spot, ws_send.at[g, o], ws_recv.at[g, o], sibling
-        )
+        return remote(spot, spot, ws_send.at[g, o], ws_recv.at[g, o], sibling)
 
     def w_begin(g):
         @pl.when(has_left)
@@ -239,7 +260,7 @@
         def _():
             w_right(g, 0).start()
 
-        w_sib(g, p, True).start()
+        w_sib(g, p).start()
 
     def w_step(g, s):
         @pl.when(p >= s)
@@ -277,9 +298,6 @@
 
         for o in range(line):
             w_sib(g, o).wait_send()
-            spot = wbuf.at[g, 2 * o + 1 - c]
-            remote(spot, spot, ws_send.at[g, o], ws_recv.at[g, o], sibling).wait_recv()
-        pltpu.make_async_copy(win.at[g], wbuf.at[g, dp], loc_sem.at[g]).wait()
 
     def x_spot(t):
         return xall.at[pl.ds(pl.multiple_of(t * share, 16), share)]
@@ -292,7 +310,7 @@
             x_copy(r).wait_send()
             spot = x_spot(lax.rem(ten + t_count - r, t_count))
             remote(spot, spot, x_send.at[r - 1], x_recv.at[r - 1], peer(r)).wait_recv()
-        pltpu.make_async_copy(xin, x_spot(ten), loc_sem.at[groups]).wait()
+        pltpu.make_async_copy(xin, x_spot(ten), loc_sem.at[groups, 0]).wait()
 
     def t_copy(r, part):
         spot = pl.ds(part * tile, tile)
@@ -304,12 +322,15 @@
             peer(r),
         )
 
+    for copy in own_copies(0):
+        copy.wait()
     w_begin(0)
+    for g in range(1, groups):
+        for copy in own_copies(g):
+            copy.wait()
     for r in range(1, t_count):
         x_copy(r).start()
-    for g in range(groups):
-        pltpu.make_async_copy(win.at[g], wbuf.at[g, dp], loc_sem.at[g]).start()
-    pltpu.make_async_copy(xin, x_spot(ten), loc_sem.at[groups]).start()
+    pltpu.make_async_copy(xin, x_spot(ten), loc_sem.at[groups, 0]).start()
 
     tiles = t_count * (cols // tile)
     deep = proj.shape[0]
@@ -366,8 +387,6 @@
             t_copy(r, part).start()
     for s in range(2, line - 1):
         w_step(0, s)
-    if groups > 1:
-        w_begin(1)
     x_wait()
 
     def x_turned(d):
@@ -381,17 +400,29 @@
         return xall[:, lanes(d * rows, rows)]
 
     lax.fori_loop(0, dp_count, turn, 0)
-    if line > 2:
-        w_step(0, line - 1)
+
+    def absorb(g, begin, end):
+        def one(o, carry):
+            spot = wbuf.at[g, 2 * o + 1 - c]
+            remote(spot, spot, ws_send.at[g, o], ws_recv.at[g, o], sibling).wait_recv()
+            acc[...] += dot(x_cols(2 * o), wbuf[g, 2 * o])
+            acc[...] += dot(x_cols(2 * o + 1), wbuf[g, 2 * o + 1])
+            return carry
+
+        lax.fori_loop(begin, end, one, 0)
+
+    near = jnp.maximum(p - (line - 2), 0)
+    far = jnp.minimum(p + (line - 2), line - 1) + 1
 
     def project(g):
-        acc[...] = dot(x_cols(0), wbuf[g, 0])
-
-        def one(d, carry):
-            acc[...] += dot(x_cols(d), wbuf[g, d])
-            return carry
-
-        lax.fori_loop(1, dp_count, one, 0)
+        acc[...] = jnp.zeros_like(acc)
+        absorb(g, near, far)
+        w_step(g, line - 1)
+        if g + 1 < groups:
+            w_begin(g + 1)
+        absorb(g, 0, near)
+        absorb(g, far, line)
+        w_finish(g)
         qkv[...] = acc[...].astype(jnp.bfloat16)
 
     def heads(g, begin, end):
@@ -419,11 +450,15 @@
 
         lax.fori_loop(begin, end, one, 0)
 
-    early = ratio - 1
+    def early(g):
+        return ratio - 1 if g == groups - 1 else ratio // 2
+
+    def part_cols(q):
+        first = early(q // 2) * HEAD
+        return pl.ds(first, width - first) if q % 2 else pl.ds(0, first)
 
     def cut(ref, q, i):
-        spot = pl.ds(0, early * HEAD) if q % 2 == 0 else pl.ds(early * HEAD, 3 * HEAD)
-        return ref.at[q // 2, i, :, spot]
+        return ref.at[q // 2, i, :, part_cols(q)]
 
     def g_sib(q, o):
         return remote(
@@ -475,9 +510,7 @@
         if q % 2:
             for j in range(2):
                 grads[:, pl.ds((ratio + j) * HEAD, HEAD)] = gkv[j].astype(jnp.bfloat16)
-            spot = pl.ds(early * HEAD, 3 * HEAD)
-        else:
-            spot = pl.ds(0, early * HEAD)
+        spot = part_cols(q)
 
         def one(i, carry):
             o = jnp.where(i % 2 == 0, line - 1 - i // 2, i // 2)
@@ -522,8 +555,7 @@
             g_left(q, k).start()
 
     def finish(q):
-        spot = pl.ds(0, early * HEAD) if q % 2 == 0 else pl.ds(early * HEAD, 3 * HEAD)
-        total = out.at[q // 2, :, spot]
+        total = out.at[q // 2, :, part_cols(q)]
         total[...] = pair(q, p)
 
         @pl.when(has_left)
@@ -548,20 +580,9 @@
             g_sib(q, o).wait_send()
 
     links = range(line - 2)
+    work = []
     for g in range(groups):
-        work = []
-        if g:
-            for q in (2 * g - 2, 2 * g - 1):
-                work += [functools.partial(chain, q, k) for k in links]
-            work += [functools.partial(finish, 2 * g - 2), functools.partial(finish, 2 * g - 1)]
-        ahead = []
-        if g + 1 < groups:
-            ahead = [functools.partial(w_step, g + 1, s) for s in range(1, line)]
-            if g > 0:
-                w_begin(g + 1)
-        w_finish(g)
-        if work:
-            work.pop(0)()
+        last = g == groups - 1
         project(g)
         gkv[...] = jnp.zeros_like(gkv)
         for part in range(cols // tile):
@@ -569,23 +590,29 @@
                 for r in range(1, t_count):
                     t_copy(r, part).wait()
         for j in range(ratio):
-            if work:
+            if j < len(links) and work:
                 work.pop(0)()
-            if ahead and j % 2 == 0 and len(ahead) > 1:
-                ahead.pop(0)()
             heads(g, j, j + 1)
-            if j == early - 1:
+            if j == early(g) - 1:
                 products(2 * g)
+                if not last:
+                    w_step(g + 1, 1)
+        if not last:
+            for k in links:
+                chain(2 * g, k)
         products(2 * g + 1)
+        if last:
+            for k in links:
+                chain(2 * g, k)
         while work:
             work.pop(0)()
-        while ahead:
-            ahead.pop(0)()
-    for q in (2 * groups - 2, 2 * groups - 1):
-        for k in links:
-            chain(q, k)
-    for q in (2 * groups - 2, 2 * groups - 1):
-        finish(q)
+        if not last:
+            for s in range(2, line - 1):
+                w_step(g + 1, s)
+        work = [functools.partial(chain, 2 * g + 1, k) for k in links]
+        work += [functools.partial(finish, 2 * g), functools.partial(finish, 2 * g + 1)]
+    while work:
+        work.pop(0)()
 
 
 def fused_call(tq, tk, tv, projector, xin, query_weight, key_weight, value_weight):
@@ -598,14 +625,6 @@
     per = q_cols // groups
     width = per + 2 * HEAD
     length = tq.shape[0]
-    win = jnp.concatenate(
-        [
-            query_weight.reshape(rows, groups, per),
-            key_weight.reshape(rows, groups, HEAD),
-            value_weight.reshape(rows, groups, HEAD),
-        ],
-        axis=2,
-    ).transpose(1, 0, 2)
     cols = projector.shape[1] // t_count
     tile = min(per, cols)
     bf = jnp.bfloat16
@@ -615,7 +634,7 @@
     out = pl.pallas_call(
         functools.partial(fused, dp_count, t_count),
         out_shape=jax.ShapeDtypeStruct((groups, rows, width), jnp.float32),
-        in_specs=[vmem, vmem, vmem, hbm, hbm, hbm],
+        in_specs=[vmem, vmem, vmem] + [hbm] * 5,
         out_specs=vmem,
         scratch_shapes=[
             pltpu.VMEM((groups, dp_count, rows, width), bf),
@@ -631,7 +650,7 @@
             pltpu.VMEM((length, width), bf),
             pltpu.VMEM((length, width), bf),
             pltpu.VMEM((2, length, HEAD), jnp.float32),
-            sem((groups + 1,)),
+            sem((groups + 1, 3)),
             sem((2,)),
             sem((t_count - 1,)),
             sem((t_count - 1,)),
@@ -643,7 +662,7 @@
         compiler_params=pltpu.CompilerParams(
             collective_id=0, has_side_effects=True, vmem_limit_bytes=VMEM_LIMIT
         ),
-    )(tq, tk, tv, projector, xin, win)
+    )(tq, tk, tv, projector, xin, query_weight, key_weight, value_weight)
     return (
         jnp.concatenate([out[g, :, :per] for g in range(groups)], axis=1),
         jnp.concatenate([out[g, :, per : per + HEAD] for g in range(groups)], axis=1),

time: 228 us -> 223 us (0.978); the launches traced: 227 us -> 218 us
  Pallas kernels: 218 us -> 214 us
  local copies, waits for them, and re-layouts: 4.5 us -> 1.73 us
    pallas_call x1, Pallas kernels: 218 us -> 214 us  [fused_call(): pl.pallas_call(functools.partial(fused, dp_count, t_count), out_shape=jax...]
where the time goes in v3:
time: 223 us; the launch traced here: 218 us
  Pallas kernels  214 us (96%)
  other arithmetic  2.55 us (1%)
    pallas_call x1, Pallas kernels, fused_call(): pl.pallas_call(functools.partial(fused, dp_count, t_count), out_shape=jax...  214 us

profile of v3, /device:TPU:0, one launch (start us, length us, event | category | flops | bytes accessed | tf_op | source)
XLA Modules:
  0.0 218.5 jit_solution(7371615670201407865)
XLA Ops:
  0.6 213.5 %shard_map.103 = f32[2,512,768]{2,1,0:T(8,128)} custom-call(bf16[512,2048]{1,0:T(8,128)(2,1)} %bitcast.16, bf16[512,256]{1,0:T(8,128)(2,1)} %bitcast.18, bf16[512,256]{1,0:T(8,128)(2,1)} %bitcast.19, bf16[2048,4096]{1,0:T(8,128)(2,1)} %proj.1, bf16[128,4096]{1,0:T(8,128)(2,1)} %bitcast.17, bf16[512,1024]{1,0:T(8,128)(2,1)} %qw.1, bf16[512,256]{1,0:T(8,128)(2,1)} %kw.1, ...), custom_call_target="tpu_custom_call" | custom-call | tf_op jit(solution)/shard_map/pallas_call | solution.py:634
  214.2 0.0 copy-start
  214.2 1.4 slice_bitcast_fusion.3
  215.6 1.0 pad_maximum_fusion.1
  216.6 0.0 copy-done
  216.6 0.3 slice_bitcast_fusion.1
  216.9 1.5 pad_maximum_fusion
Async XLA Ops:
  214.2 2.5 %copy-start = (f32[2,512,768]{2,1,0:T(8,128)S(1)}, f32[2,512,768]{2,1,0:T(8,128)}, u32[]{:S(2)}) copy-start(f32[2,512,768]{2,1,0:T(8,128)} %shard_map.103) | copy-start | bytes 9437188

commit v4 on v3

--- a/solution.py
+++ b/solution.py
@@ -371,9 +371,9 @@
             ).astype(jnp.bfloat16)
         return carry
 
-    lax.fori_loop(0, 3 * t_heads // 4, teacher_head, 0)
+    lax.fori_loop(0, 3 * t_heads // 4, teacher_head, 0, unroll=2)
     w_step(0, 1)
-    lax.fori_loop(3 * t_heads // 4, t_heads, teacher_head, 0)
+    lax.fori_loop(3 * t_heads // 4, t_heads, teacher_head, 0, unroll=2)
     for i in range(tiles):
         tile_copy(i).wait()
         r = (1 + i) % t_count
@@ -383,7 +383,7 @@
         )
         if i + 2 < tiles:
             tile_copy(i + 2).start()
-        if r:
+        if r and part == 0:
             t_copy(r, part).start()
     for s in range(2, line - 1):
         w_step(0, s)
@@ -589,6 +589,9 @@
             if (part * tile) // (ratio * HEAD) == g:
                 for r in range(1, t_count):
                     t_copy(r, part).wait()
+                if part + 1 < cols // tile:
+                    for r in range(1, t_count):
+                        t_copy(r, part + 1).start()
         for j in range(ratio):
             if j < len(links) and work:
                 work.pop(0)()

time: 223 us -> 223 us (level)
  no operation moved by 1% of the time
where the time goes in v4:
time: 223 us; the launch traced here: 220 us
  Pallas kernels  215 us (96%)
  other arithmetic  2.55 us (1%)
    pallas_call x1, Pallas kernels, fused_call(): pl.pallas_call(functools.partial(fused, dp_count, t_count), out_shape=jax...  215 us

profile of v4, /device:TPU:0, one launch (start us, length us, event | category | flops | bytes accessed | tf_op | source)
XLA Modules:
  0.0 220.2 jit_solution(13116344658883825532)
XLA Ops:
  0.6 215.3 %shard_map.103 = f32[2,512,768]{2,1,0:T(8,128)} custom-call(bf16[512,2048]{1,0:T(8,128)(2,1)} %bitcast.16, bf16[512,256]{1,0:T(8,128)(2,1)} %bitcast.18, bf16[512,256]{1,0:T(8,128)(2,1)} %bitcast.19, bf16[2048,4096]{1,0:T(8,128)(2,1)} %proj.1, bf16[128,4096]{1,0:T(8,128)(2,1)} %bitcast.17, bf16[512,1024]{1,0:T(8,128)(2,1)} %qw.1, bf16[512,256]{1,0:T(8,128)(2,1)} %kw.1, ...), custom_call_target="tpu_custom_call" | custom-call | tf_op jit(solution)/shard_map/pallas_call | solution.py:637
  215.9 0.0 copy-start
  215.9 1.4 slice_bitcast_fusion.3
  217.4 1.0 pad_maximum_fusion.1
  218.4 0.0 copy-done
  218.4 0.3 slice_bitcast_fusion.1
  218.7 1.5 pad_maximum_fusion
Async XLA Ops:
  215.9 2.5 %copy-start = (f32[2,512,768]{2,1,0:T(8,128)S(1)}, f32[2,512,768]{2,1,0:T(8,128)}, u32[]{:S(2)}) copy-start(f32[2,512,768]{2,1,0:T(8,128)} %shard_map.103) | copy-start | bytes 9437188
